TPU v7x, 128 devices: a whole 4x4x4 slice. The times are simulated.
128 devices in a mesh: dp: 32 (over z, y, core), mp: 4 (over x).
Axes of the slice: x: 4, y: 4, z: 4, core: 2. Of those that a mesh axis runs over, the one named last changes fastest.
Arguments:
- patches: bfloat16 [49152, 128], P(('dp', 'mp')), may hold values from -6 to 6
- row_count: int32 [128], P(('dp', 'mp')), may hold values from 0 to 384, as said below
- target_group: int32 [49152], P(('dp', 'mp')), may hold values from 0 to 31, as said below
- target_offset: int32 [49152], P(('dp', 'mp')), may hold values from 0 to 639, as said below
- embed: bfloat16 [128, 6144], replicated, may hold values from -0.5 to 0.5
- norm_gain: bfloat16 [6144], replicated, may hold values from 0.099609375 to 1.8984375
- readout: bfloat16 [6144, 128], P('mp'), may hold values from -0.078125 to 0.078125
- target: bfloat16 [20480, 128], P('dp'), may hold values from -12 to 12
- master: float32 [6144, 6144], P('dp', 'mp'), may hold values from -6 to 6
- moment1: float32 [6144, 6144], P('dp', 'mp'), may hold values from -2 to 2
- moment2: float32 [6144, 6144], P('dp', 'mp'), may hold values from 0.0034722222 to 0.1388889
Outputs:
- prediction: float32 [20480, 128], P('dp')
- master_new: float32 [6144, 6144], P('dp', 'mp')
- moment1_new: float32 [6144, 6144], P('dp', 'mp')
- moment2_new: float32 [6144, 6144], P('dp', 'mp')
- weight_copy: bfloat16 [6144, 6144], P('dp', 'mp')
Inputs may be any that keep to these rules, and one draw needn't show every extreme that they name: Device i holds its live patch rows in its first row_count[i] slots; some device holds 384 of them in every draw. Over the live slots of all devices, each pair (target_group, target_offset) of the 20480 positions occurs exactly once; values in slots past row_count are arbitrary within the range. Call target_offset // 160 the block of a row. Each (batch, block) receives exactly 160 live rows; one device sends at most 3 live rows to one (batch, block), and every (batch, block) gets 3 rows from some device.
All inputs are finite; a program needn't handle non-finite values.
Results may differ from a plain program's by a relative error of at most 0.03.
Values may be sent and summed in bfloat16 or wider, within the bound.
A program may use at most 128 MiB of HBM per device.

v0:
```python
import jax
import jax.numpy as jnp
from jax import lax
from jax.sharding import PartitionSpec as P

gelu_const = 0.7978845608028654
beta_one = 0.9
beta_two = 0.95
learn_rate = 0.01
decay_rate = 0.1
adam_epsilon = 1e-08
step_count = 20


def gelu_tanh(value):
    inner = gelu_const * (value + 0.044715 * value * value * value)
    return 0.5 * value * (1.0 + jnp.tanh(inner))


def gelu_slope(value):
    tangent = jnp.tanh(gelu_const * (value + 0.044715 * value * value * value))
    return 0.5 * (1.0 + tangent) + 0.5 * value * (1.0 - tangent * tangent) * gelu_const * (
        1.0 + 3.0 * 0.044715 * value * value
    )


def shards(
    patches,
    row_count,
    target_group,
    target_offset,
    embed,
    norm_gain,
    readout,
    target,
    master,
    moment1,
    moment2,
):
    model_count = lax.axis_size("mp")
    batch_count = lax.axis_size("dp")
    devices_all = batch_count * model_count
    slot_total = patches.shape[0]
    capacity = slot_total // devices_all
    batch_rows = target.shape[0]
    block_rows = batch_rows // model_count
    width = embed.shape[1]
    patch_width = patches.shape[1]
    occupied = jnp.arange(slot_total, dtype=jnp.int32) < row_count[0]
    owner_index = jnp.where(
        occupied, target_group * model_count + target_offset // block_rows, devices_all
    )
    onehot = (owner_index[:, None] == jnp.arange(devices_all, dtype=jnp.int32)[None, :]).astype(
        jnp.int32
    )
    running = jnp.cumsum(onehot, axis=0)
    placing = jnp.sum(onehot * running, axis=1) - 1
    send_slot = jnp.where(occupied, owner_index * capacity + placing, devices_all * capacity)
    outgoing = (
        jnp.zeros((devices_all * capacity, patch_width), jnp.bfloat16)
        .at[send_slot]
        .set(patches, mode="drop")
    )
    slot_marks = (
        jnp.full((devices_all * capacity,), block_rows, jnp.int32)
        .at[send_slot]
        .set(target_offset % block_rows, mode="drop")
    )
    arrived, arrived_marks = (
        lax.all_to_all(outgoing, ("dp", "mp"), split_axis=0, concat_axis=0, tiled=True),
        lax.all_to_all(slot_marks, ("dp", "mp"), split_axis=0, concat_axis=0, tiled=True),
    )
    block_patches = (
        jnp.zeros((block_rows, patch_width), jnp.bfloat16)
        .at[arrived_marks]
        .set(arrived, mode="drop")
    )
    gain_wide = norm_gain.astype(jnp.float32)
    hidden = gelu_tanh(
        jnp.dot(
            lax.all_gather(block_patches, "mp", axis=0, tiled=True),
            embed,
            preferred_element_type=jnp.float32,
        )
    )
    normed = (
        hidden * lax.rsqrt(jnp.mean(hidden * hidden, axis=-1, keepdims=True) + 1e-05) * gain_wide
    ).astype(jnp.bfloat16)
    weight = master.astype(jnp.bfloat16)
    width_scale = 1.0 / width**0.5
    columns = normed
    preact = (
        jnp.dot(
            columns,
            lax.all_gather(weight, "dp", axis=0, tiled=True),
            preferred_element_type=jnp.float32,
        )
        * width_scale
    )
    activation = gelu_tanh(preact).astype(jnp.bfloat16)
    prediction = lax.psum(
        jnp.dot(activation, readout, preferred_element_type=jnp.float32).astype(jnp.bfloat16), "mp"
    ).astype(jnp.float32)
    errors = (prediction - target.astype(jnp.float32)).astype(jnp.bfloat16)
    backward = lax.dot_general(
        errors, readout, (((1,), (1,)), ((), ())), preferred_element_type=jnp.float32
    )
    delta_rows = (backward * gelu_slope(preact)).astype(jnp.bfloat16)
    columns = normed
    gradient = lax.psum_scatter(
        (
            lax.dot_general(
                columns, delta_rows, (((0,), (0,)), ((), ())), preferred_element_type=jnp.float32
            )
            * width_scale
        ).astype(jnp.bfloat16),
        "dp",
        scatter_dimension=0,
        tiled=True,
    ).astype(jnp.float32)
    moment1_new = beta_one * moment1 + (1.0 - beta_one) * gradient
    moment2_new = beta_two * moment2 + (1.0 - beta_two) * gradient * gradient
    first_fix = moment1_new / (1.0 - beta_one**step_count)
    second_fix = moment2_new / (1.0 - beta_two**step_count)
    master_new = master - learn_rate * (
        first_fix / (jnp.sqrt(second_fix) + adam_epsilon) + decay_rate * master
    )
    return (prediction, master_new, moment1_new, moment2_new, master_new.astype(jnp.bfloat16))


def solution(mesh):
    placed = (
        P(("dp", "mp"), None),
        P(("dp", "mp")),
        P(("dp", "mp")),
        P(("dp", "mp")),
        P(),
        P(),
        P("mp", None),
        P("dp", None),
        P("dp", "mp"),
        P("dp", "mp"),
        P("dp", "mp"),
    )
    return jax.shard_map(
        shards,
        mesh=mesh,
        in_specs=placed,
        out_specs=(P("dp", None), P("dp", "mp"), P("dp", "mp"), P("dp", "mp"), P("dp", "mp")),
        check_vma=False,
    )
```

profile of v0, /device:TPU:0, one launch (start us, length us, event | category | flops | bytes accessed | tf_op | source)
XLA Modules:
  0.0 316.7 jit_solution(15524870666545750787)
XLA Ops:
  7.2 0.0 copy-start
  7.2 0.0 copy-start.4
  7.2 0.0 all-gather.2.cloned.1.call-start
  7.2 2.3 convert_element_type.44
  9.5 0.0 all-gather.2.cloned.1.call-update
  10.2 0.7 add_select_fusion
  10.9 0.1 copy.18
  11.0 0.2 fusion.14
  11.3 0.1 broadcast_add_fusion
  11.3 0.2 fusion.16
  11.6 2.9 scatter_custom_fusion
  14.5 0.8 all_to_all.16
  15.3 11.1 %all-to-all-start = ((s32[128,3,1]{1,2,0:T(1,128)}), s32[128,3,1]{1,2,0:T(1,128)S(1)}, u32[]{:S(2)}, u32[]{:S(2)}) async-start(s32[128,3,1]{1,2,0:T(1,128)} %bitcast.5), calls=%async_computation | async-start | bytes 131072 | tf_op jit(solution)/shard_map/all_to_all | solution.py:71
  26.5 0.0 copy-done.4
  26.5 1.8 scatter_custom_fusion.1
  28.3 0.7 all_to_all.19
  29.0 6.7 %all-to-all-done = s32[128,3,1]{1,2,0:T(1,128)S(1)} async-done(((s32[128,3,1]{1,2,0:T(1,128)}), s32[128,3,1]{1,2,0:T(1,128)S(1)}, u32[]{:S(2)}, u32[]{:S(2)}) %all-to-all-start) | async-done | bytes 1568 | tf_op jit(solution)/shard_map/all_to_all | solution.py:71
  35.7 4.6 %all-to-all-start.1 = ((bf16[128,3,128]{2,1,0:T(4,128)(2,1)}), bf16[128,3,128]{2,1,0:T(4,128)(2,1)S(1)}, u32[]{:S(2)}, u32[]{:S(2)}) async-start(bf16[128,3,128]{2,1,0:T(4,128)(2,1)} %all_to_all.19), calls=%async_computation.1 | async-start | bytes 262144 | tf_op jit(solution)/shard_map/all_to_all | solution.py:70
  40.4 0.0 all-reduce.2.cloned.1.call-start
  40.4 0.5 broadcast.113
  40.9 0.8 reduce.5
  41.7 0.2 all_to_all.18
  42.0 7.9 %all-to-all-done.1 = bf16[128,3,128]{2,1,0:T(4,128)(2,1)S(1)} async-done(((bf16[128,3,128]{2,1,0:T(4,128)(2,1)}), bf16[128,3,128]{2,1,0:T(4,128)(2,1)S(1)}, u32[]{:S(2)}, u32[]{:S(2)}) %all-to-all-start.1) | async-done | bytes 98336 | tf_op jit(solution)/shard_map/all_to_all | solution.py:70
  49.8 0.1 reshape.88
  49.9 1.4 scatter_custom_fusion.2
  51.4 12.2 %all_gather.6 = bf16[640,128]{1,0:T(8,128)(2,1)S(1)} all-gather(bf16[160,128]{1,0:T(8,128)(2,1)S(1)} %scatter_custom_fusion.2), channel_id=1, replica_groups=mesh['dp'=32,'mp'=4] {'mp'}, dimensions={0}, use_global_device_ids=true | all-gather | bytes 204800 | tf_op jit(solution)/shard_map/all_gather | solution.py:81
  63.6 0.0 copy-done
  63.6 9.0 %multiply_reduce_fusion = (f32[640]{0:T(1024)S(1)}, f32[640,6144]{1,0:T(8,128)}) fusion(bf16[640,128]{1,0:T(8,128)(2,1)S(1)} %all_gather.6, bf16[128,6144]{1,0:T(8,128)(2,1)S(1)} %copy-done), kind=kOutput, calls=%fused_computation.10 | convolution fusion | flops 1045953920 | bytes 17467904 | tf_op jit(solution)/shard_map/dot_general | solution.py:80
  72.6 19.0 %all-gather.2.cloned.1.call-done = bf16[6144,1536]{1,0:T(8,128)(2,1)} async-done(((bf16[192,1536]{1,0:T(8,128)(2,1)}), bf16[6144,1536]{1,0:T(8,128)(2,1)}) %all-gather.2.cloned.1.call-update) | async-done | bytes 18874384 | tf_op jit(solution)/shard_map/all_gather | solution.py:95
  91.6 0.0 copy-start.5
  91.6 18.6 %fusion.40 = f32[640,1536]{1,0:T(8,128)S(1)} fusion(bf16[6144,1536]{1,0:T(8,128)(2,1)} %all-gather.2.cloned.1.call-done, f32[640,6144]{1,0:T(8,128)} %get-tuple-element.12, f32[6144]{0:T(1024)S(1)} %convert_element_type.42, f32[640]{0:T(1024)S(1)} %add_rsqrt_fusion), kind=kOutput, calls=%fused_computation.67 | convolution fusion | flops 12091392000 | bytes 38562304 | tf_op jit(solution)/shard_map/dot_general | solution.py:93
  110.2 0.0 copy-start.7
  110.2 2.0 copy-done.7
  112.2 0.0 copy-done.5
  112.2 0.0 copy-start.6
  112.2 2.2 fusion.13
  114.4 0.0 all-reduce.2.cloned.1.call-update
  114.4 0.3 reduce-scatter.2.cloned.1.call-start
  114.7 40.5 %all-reduce.2.cloned.1.call-done = bf16[640,128]{1,0:T(8,128)(2,1)} async-done(((bf16[640,128]{1,0:T(8,128)(2,1)}), bf16[640,128]{1,0:T(8,128)(2,1)}) %all-reduce.2.cloned.1.call-update) | async-done | bytes 163856 | tf_op jit(solution)/shard_map/psum | solution.py:101
  155.2 0.9 convert_element_type.47
  156.1 0.0 copy-done.6
  156.1 0.0 copy-start.3
  156.1 27.2 %multiply_convert_fusion = bf16[6144,1536]{1,0:T(8,128)(2,1)} fusion(f32[640,1536]{1,0:T(8,128)} %copy-done.7, bf16[1536,128]{1,0:T(8,128)(2,1)S(1)} %copy-done.5, f32[640,128]{1,0:T(8,128)S(1)} %convert_element_type.47, bf16[640,128]{1,0:T(8,128)(2,1)S(1)} %copy-done.6, f32[640,6144]{1,0:T(8,128)} %get-tuple-element.12, f32[6144]{0:T(1024)S(1)} %convert_element_type.42, ...), kind=kOutput, calls=%fused_computation.3 | convolution fusion | flops 12381831168 | bytes 39447040 | tf_op jit(solution)/shard_map/dot_general | solution.py:112
  183.4 0.0 copy-done.3
  183.4 0.0 copy-start.2
  183.4 0.0 reduce-scatter.2.cloned.1.call-update
  183.4 0.0 copy-start.1
  183.4 122.3 %reduce-scatter.2.cloned.1.call-done = bf16[192,1536]{1,0:T(8,128)(2,1)} async-done(((bf16[6144,1536]{1,0:T(8,128)(2,1)}), bf16[192,1536]{1,0:T(8,128)(2,1)}) %reduce-scatter.2.cloned.1.call-update) | async-done | bytes 589840 | tf_op jit(solution)/shard_map/reduce_scatter | solution.py:110
  305.7 0.0 copy-done.2
  305.7 4.4 %fusion.41 = (bf16[192,1536]{1,0:T(8,128)(2,1)}, f32[192,1536]{1,0:T(8,128)}, f32[192,1536]{1,0:T(8,128)}, f32[192,1536]{1,0:T(8,128)}) fusion(f32[192,1536]{1,0:T(8,128)S(1)} %copy-done.2, bf16[192,1536]{1,0:T(8,128)(2,1)} %reduce-scatter.2.cloned.1.call-done, f32[192,1536]{1,0:T(8,128)} %param.20, f32[192,1536]{1,0:T(8,128)} %param.21), kind=kLoop, calls=%fused_computation.68 | loop fusion | flops 5013504 | bytes 8257536 | tf_op jit(solution)/shard_map/convert_element_type | solution.py:128
  310.1 0.0 copy-done.1
  (7 shorter events, 0.1 us)
Async XLA Ops:
  7.2 56.4 %copy-start = (bf16[128,6144]{1,0:T(8,128)(2,1)S(1)}, bf16[128,6144]{1,0:T(8,128)(2,1)}, u32[]{:S(2)}) copy-start(bf16[128,6144]{1,0:T(8,128)(2,1)} %param.15) | copy-start | bytes 4718596
  7.2 19.3 %copy-start.4 = (bf16[6144]{0:T(1024)(128)(2,1)S(1)}, bf16[6144]{0:T(1024)(128)(2,1)}, u32[]{:S(2)}) copy-start(bf16[6144]{0:T(1024)(128)(2,1)} %param.16) | copy-start | bytes 36868
  7.2 84.4 %all-gather.2.cloned.1.call-start = ((), (), s32[]{:S(2)}) async-start(), calls=%async_computation.3 | async-start | bytes 19464192 | tf_op jit(solution)/shard_map/all_gather | solution.py:95
  15.3 20.4 %all-to-all-start = ((s32[128,3,1]{1,2,0:T(1,128)}), s32[128,3,1]{1,2,0:T(1,128)S(1)}, u32[]{:S(2)}, u32[]{:S(2)}) async-start(s32[128,3,1]{1,2,0:T(1,128)} %bitcast.5), calls=%async_computation | async-start | bytes 131072 | tf_op jit(solution)/shard_map/all_to_all | solution.py:71
  35.7 14.1 %all-to-all-start.1 = ((bf16[128,3,128]{2,1,0:T(4,128)(2,1)}), bf16[128,3,128]{2,1,0:T(4,128)(2,1)S(1)}, u32[]{:S(2)}, u32[]{:S(2)}) async-start(bf16[128,3,128]{2,1,0:T(4,128)(2,1)} %all_to_all.19), calls=%async_computation.1 | async-start | bytes 262144 | tf_op jit(solution)/shard_map/all_to_all | solution.py:70
  40.4 114.8 %all-reduce.2.cloned.1.call-start = ((), (), s32[]{:S(2)}) async-start(), calls=%async_computation.4 | async-start | bytes 327680 | tf_op jit(solution)/shard_map/psum | solution.py:101
  91.6 20.6 %copy-start.5 = (bf16[1536,128]{1,0:T(8,128)(2,1)S(1)}, bf16[1536,128]{1,0:T(8,128)(2,1)}, u32[]{:S(2)}) copy-start(bf16[1536,128]{1,0:T(8,128)(2,1)} %param.17) | copy-start | bytes 1179652
  110.2 2.0 copy-start.7
  112.2 43.9 %copy-start.6 = (bf16[640,128]{1,0:T(8,128)(2,1)S(1)}, bf16[640,128]{1,0:T(8,128)(2,1)}, u32[]{:S(2)}) copy-start(bf16[640,128]{1,0:T(8,128)(2,1)} %param.18) | copy-start | bytes 491524
  114.4 191.3 %reduce-scatter.2.cloned.1.call-start = ((), (), s32[]{:S(2)}) async-start(), calls=%async_computation.5 | async-start | bytes 19464192 | tf_op jit(solution)/shard_map/reduce_scatter | solution.py:110
  156.1 27.3 %copy-start.3 = (f32[640,128]{1,0:T(8,128)}, f32[640,128]{1,0:T(8,128)S(1)}, u32[]{:S(2)}) copy-start(f32[640,128]{1,0:T(8,128)S(1)} %convert_element_type.47) | copy-start | bytes 983044
  183.4 122.3 %copy-start.2 = (f32[192,1536]{1,0:T(8,128)S(1)}, f32[192,1536]{1,0:T(8,128)}, u32[]{:S(2)}) copy-start(f32[192,1536]{1,0:T(8,128)} %param.19) | copy-start | bytes 3538948
  183.4 126.7 %copy-start.1 = (bf16[128,6144]{1,0:T(8,128)(2,1)S(1)}, bf16[128,6144]{1,0:T(8,128)(2,1)}, u32[]{:S(2)}) copy-start(bf16[128,6144]{1,0:T(8,128)(2,1)} %param.15) | copy-start | bytes 4718596
Sparse Core Ops, SparseCore 0:
  10.9 80.6 all-gather.1
  114.5 40.6 all-reduce.1
  183.5 122.1 reduce-scatter.1
where the time goes:
time: 317 us
  waiting for transfers between devices  196 us (62%)
  matrix products  57 us (18%)
  starting transfers between devices  16.1 us (5%)
  between operations  14.6 us (5%)
  blocking collectives  12.2 us (4%)
  local copies, waits for them, and re-layouts  10.7 us (3%)
  other arithmetic  9.67 us (3%)
    reduce_scatter x1, waiting for transfers between devices, shards(): lax.psum_scatter((lax.dot_general(columns, delta_rows, (((0,), (0,)), (()...  122 us
    psum x1, waiting for transfers between devices, shards(): lax.psum(jnp.dot(activation, readout, preferred_element_type=jnp.float32)...  40.5 us
    dot_general x1, matrix products, shards(): lax.dot_general(columns, delta_rows, (((0,), (0,)), ((), ())), preferred_...  27.2 us
    all_gather x1, waiting for transfers between devices, shards(): lax.all_gather(weight, 'dp', axis=0, tiled=True)  19 us
    dot_general x1, matrix products, shards(): jnp.dot(columns, lax.all_gather(weight, 'dp', axis=0, tiled=True), prefer...  18.6 us
    all_gather x1, blocking collectives, shards(): lax.all_gather(block_patches, 'mp', axis=0, tiled=True)  12.2 us
    all_to_all x1, starting transfers between devices, shards(): lax.all_to_all(slot_marks, ('dp', 'mp'), split_axis=0, concat_axis=0, til...  11.1 us
    dot_general x1, matrix products, shards(): jnp.dot(lax.all_gather(block_patches, 'mp', axis=0, tiled=True), embed, p...  8.99 us
  transfers between devices with their start and end apart: 5, of which 5 were waited for; matrix products, arithmetic and copies ran while one was open for 6% of the time, Pallas kernels for 0%

commit v1 on v0

--- a/solution.py
+++ b/solution.py
@@ -92,7 +92,9 @@
     preact = (
         jnp.dot(
             columns,
-            lax.all_gather(weight, "dp", axis=0, tiled=True),
+            jnp.concatenate(
+                lax.all_to_all(jnp.stack([weight] * lax.axis_size("dp")), "dp", 0, 0), axis=0
+            ),
             preferred_element_type=jnp.float32,
         )
         * width_scale

time: 317 us -> 522 us (1.65)
  waiting for transfers between devices: 196 us -> 390 us
  local copies, waits for them, and re-layouts: 10.7 us -> 17.4 us
  starting transfers between devices: 16.1 us -> 21.4 us
    all_to_all x0 -> x1, waiting for transfers between devices: none -> 217 us  [shards(): lax.all_to_all(jnp.stack([weight] * lax.axis_size('dp')), 'dp', 0, 0)]
    all_gather x1 -> x0, waiting for transfers between devices: 19 us -> none  [shards(): lax.all_gather(weight, 'dp', axis=0, tiled=True)]
    another operation x2 -> x3, local copies, waits for them, and re-layouts: 0.02 us -> 6.78 us  [the longest x1 6.76 us: shards(): jnp.stack([weight] * lax.axis_size('dp'))]
    all_to_all x0 -> x1, starting transfers between devices: none -> 5.32 us  [shards(): lax.all_to_all(jnp.stack([weight] * lax.axis_size('dp')), 'dp', 0, 0)]
  transfers between devices with their start and end apart: 5 -> 5, of which waited for: 5 -> 5; matrix products, arithmetic and copies ran while one was open for 6% -> 3% of each run, Pallas kernels for 0% -> 0%
where the time goes in v1:
time: 522 us; the launch traced here: 521 us
  waiting for transfers between devices  390 us (75%)
  matrix products  56.9 us (11%)
  starting transfers between devices  21.4 us (4%)
  local copies, waits for them, and re-layouts  17.4 us (3%)
  between operations  15 us (3%)
  blocking collectives  12.2 us (2%)
  other arithmetic  8.74 us (2%)
    all_to_all x1, waiting for transfers between devices, shards(): lax.all_to_all(jnp.stack([weight] * lax.axis_size('dp')), 'dp', 0, 0)  217 us
    reduce_scatter x1, waiting for transfers between devices, shards(): lax.psum_scatter((lax.dot_general(columns, delta_rows, (((0,), (0,)), (()...  122 us
    psum x1, waiting for transfers between devices, shards(): lax.psum(jnp.dot(activation, readout, preferred_element_type=jnp.float32)...  35.7 us
    dot_general x1, matrix products, shards(): lax.dot_general(columns, delta_rows, (((0,), (0,)), ((), ())), preferred_...  27.2 us
    dot_general x1, matrix products, shards(): jnp.dot(columns, jnp.concatenate(lax.all_to_all(jnp.stack([weight] * lax....  18.6 us
    all_gather x1, blocking collectives, shards(): lax.all_gather(block_patches, 'mp', axis=0, tiled=True)  12.2 us
    all_to_all x1, starting transfers between devices, shards(): lax.all_to_all(slot_marks, ('dp', 'mp'), split_axis=0, concat_axis=0, til...  11.1 us
  transfers between devices with their start and end apart: 5, of which 5 were waited for; matrix products, arithmetic and copies ran while one was open for 3% of the time, Pallas kernels for 0%

profile of v1, /device:TPU:0, one launch (start us, length us, event | category | flops | bytes accessed | tf_op | source)
XLA Modules:
  0.0 521.2 jit_solution(5257630879746812408)
XLA Ops:
  7.2 0.0 copy-start
  7.9 0.7 add_select_fusion
  8.7 0.1 copy.18
  8.8 0.2 fusion.14
  9.0 0.1 broadcast_add_fusion
  9.1 0.2 fusion.16
  9.3 2.9 scatter_custom_fusion
  12.3 0.8 all_to_all.19
  13.1 11.1 %all-to-all-start = ((s32[128,3,1]{1,2,0:T(1,128)}), s32[128,3,1]{1,2,0:T(1,128)S(1)}, u32[]{:S(2)}, u32[]{:S(2)}) async-start(s32[128,3,1]{1,2,0:T(1,128)} %bitcast.5), calls=%async_computation | async-start | bytes 131072 | tf_op jit(solution)/shard_map/all_to_all | solution.py:71
  24.3 1.8 scatter_custom_fusion.1
  26.1 0.7 all_to_all.22
  26.8 6.7 %all-to-all-done = s32[128,3,1]{1,2,0:T(1,128)S(1)} async-done(((s32[128,3,1]{1,2,0:T(1,128)}), s32[128,3,1]{1,2,0:T(1,128)S(1)}, u32[]{:S(2)}, u32[]{:S(2)}) %all-to-all-start) | async-done | bytes 1568 | tf_op jit(solution)/shard_map/all_to_all | solution.py:71
  33.5 4.6 all-to-all-start.1
  38.1 1.3 convert_element_type.44
  39.5 8.1 %all-to-all-done.1 = bf16[128,3,128]{2,1,0:T(4,128)(2,1)S(1)} async-done(((bf16[128,3,128]{2,1,0:T(4,128)(2,1)}), bf16[128,3,128]{2,1,0:T(4,128)(2,1)S(1)}, u32[]{:S(2)}, u32[]{:S(2)}) %all-to-all-start.1) | async-done | bytes 98336 | tf_op jit(solution)/shard_map/all_to_all | solution.py:70
  47.6 6.8 %stack.2 = bf16[32,192,1536]{2,1,0:T(8,128)(2,1)} broadcast(bf16[192,1536]{1,0:T(8,128)(2,1)S(1)} %convert_element_type.44), dimensions={1,2} | broadcast | bytes 19464192 | tf_op jit(solution)/shard_map/stack | solution.py:96
  54.4 0.0 copy-start.4
  54.4 5.3 %all-to-all-start.2 = ((bf16[32,192,1536]{2,1,0:T(8,128)(2,1)}), bf16[32,192,1536]{2,1,0:T(8,128)(2,1)}, u32[]{:S(2)}, u32[]{:S(2)}) async-start(bf16[32,192,1536]{2,1,0:T(8,128)(2,1)} %stack.2), calls=%async_computation.2 | async-start | bytes 37748736 | tf_op jit(solution)/shard_map/all_to_all | solution.py:96
  59.7 0.0 all-reduce.2.cloned.1.call-start
  59.8 0.0 copy-done.4
  59.8 0.5 broadcast.115
  60.3 0.8 reduce.5
  61.1 0.2 all_to_all.21
  61.3 0.1 reshape.94
  61.4 1.4 scatter_custom_fusion.2
  62.9 12.2 %all_gather.3 = bf16[640,128]{1,0:T(8,128)(2,1)S(1)} all-gather(bf16[160,128]{1,0:T(8,128)(2,1)S(1)} %scatter_custom_fusion.2), channel_id=1, replica_groups=mesh['dp'=32,'mp'=4] {'mp'}, dimensions={0}, use_global_device_ids=true | all-gather | bytes 204800 | tf_op jit(solution)/shard_map/all_gather | solution.py:81
  75.1 0.0 copy-done
  75.1 8.9 %multiply_reduce_fusion = (f32[640]{0:T(1024)S(1)}, f32[640,6144]{1,0:T(8,128)}) fusion(bf16[640,128]{1,0:T(8,128)(2,1)S(1)} %all_gather.3, bf16[128,6144]{1,0:T(8,128)(2,1)S(1)} %copy-done), kind=kOutput, calls=%fused_computation.10 | convolution fusion | flops 1045953920 | bytes 17467904 | tf_op jit(solution)/shard_map/dot_general | solution.py:80
  84.0 216.7 %all-to-all-done.2 = bf16[32,192,1536]{2,1,0:T(8,128)(2,1)} async-done(((bf16[32,192,1536]{2,1,0:T(8,128)(2,1)}), bf16[32,192,1536]{2,1,0:T(8,128)(2,1)}, u32[]{:S(2)}, u32[]{:S(2)}) %all-to-all-start.2) | async-done | bytes 18874400 | tf_op jit(solution)/shard_map/all_to_all | solution.py:96
  300.7 0.0 copy-start.5
  300.7 18.6 %fusion.40 = f32[640,1536]{1,0:T(8,128)S(1)} fusion(bf16[6144,1536]{1,0:T(8,128)(2,1)} %bitcast.6, f32[640,6144]{1,0:T(8,128)} %get-tuple-element.12, f32[6144]{0:T(1024)S(1)} %convert_element_type.42, f32[640]{0:T(1024)S(1)} %add_rsqrt_fusion), kind=kOutput, calls=%fused_computation.67 | convolution fusion | flops 12091392000 | bytes 38562304 | tf_op jit(solution)/shard_map/dot_general | solution.py:93
  319.3 0.0 copy-start.7
  319.3 1.9 copy-done.7
  321.3 0.0 copy-done.5
  321.3 0.0 copy-start.6
  321.3 2.2 fusion.13
  323.4 0.0 all-reduce.2.cloned.1.call-update
  323.4 0.3 reduce-scatter.2.cloned.1.call-start
  323.7 35.7 %all-reduce.2.cloned.1.call-done = bf16[640,128]{1,0:T(8,128)(2,1)} async-done(((bf16[640,128]{1,0:T(8,128)(2,1)}), bf16[640,128]{1,0:T(8,128)(2,1)}) %all-reduce.2.cloned.1.call-update) | async-done | bytes 163856 | tf_op jit(solution)/shard_map/psum | solution.py:103
  359.4 0.9 convert_element_type.47
  360.3 0.0 copy-done.6
  360.3 0.0 copy-start.3
  360.3 27.2 %multiply_convert_fusion = bf16[6144,1536]{1,0:T(8,128)(2,1)} fusion(f32[640,1536]{1,0:T(8,128)} %copy-done.7, bf16[1536,128]{1,0:T(8,128)(2,1)S(1)} %copy-done.5, f32[640,128]{1,0:T(8,128)S(1)} %convert_element_type.47, bf16[640,128]{1,0:T(8,128)(2,1)S(1)} %copy-done.6, f32[640,6144]{1,0:T(8,128)} %get-tuple-element.12, f32[6144]{0:T(1024)S(1)} %convert_element_type.42, ...), kind=kOutput, calls=%fused_computation.3 | convolution fusion | flops 12381831168 | bytes 39447040 | tf_op jit(solution)/shard_map/dot_general | solution.py:114
  387.6 0.0 copy-done.3
  387.6 0.0 copy-start.2
  387.6 0.0 reduce-scatter.2.cloned.1.call-update
  387.6 0.0 copy-start.1
  387.6 122.3 %reduce-scatter.2.cloned.1.call-done = bf16[192,1536]{1,0:T(8,128)(2,1)} async-done(((bf16[6144,1536]{1,0:T(8,128)(2,1)}), bf16[192,1536]{1,0:T(8,128)(2,1)}) %reduce-scatter.2.cloned.1.call-update) | async-done | bytes 589840 | tf_op jit(solution)/shard_map/reduce_scatter | solution.py:112
  509.9 0.0 copy-done.2
  509.9 4.4 fusion.41
  514.3 0.0 copy-done.1
  (7 shorter events, 0.1 us)
Async XLA Ops:
  7.2 67.9 %copy-start = (bf16[128,6144]{1,0:T(8,128)(2,1)S(1)}, bf16[128,6144]{1,0:T(8,128)(2,1)}, u32[]{:S(2)}) copy-start(bf16[128,6144]{1,0:T(8,128)(2,1)} %param.15) | copy-start | bytes 4718596
  13.1 20.4 %all-to-all-start = ((s32[128,3,1]{1,2,0:T(1,128)}), s32[128,3,1]{1,2,0:T(1,128)S(1)}, u32[]{:S(2)}, u32[]{:S(2)}) async-start(s32[128,3,1]{1,2,0:T(1,128)} %bitcast.5), calls=%async_computation | async-start | bytes 131072 | tf_op jit(solution)/shard_map/all_to_all | solution.py:71
  33.5 14.1 %all-to-all-start.1 = ((bf16[128,3,128]{2,1,0:T(4,128)(2,1)}), bf16[128,3,128]{2,1,0:T(4,128)(2,1)S(1)}, u32[]{:S(2)}, u32[]{:S(2)}) async-start(bf16[128,3,128]{2,1,0:T(4,128)(2,1)} %all_to_all.22), calls=%async_computation.1 | async-start | bytes 262144 | tf_op jit(solution)/shard_map/all_to_all | solution.py:70
  54.4 5.4 %copy-start.4 = (bf16[6144]{0:T(1024)(128)(2,1)S(1)}, bf16[6144]{0:T(1024)(128)(2,1)}, u32[]{:S(2)}) copy-start(bf16[6144]{0:T(1024)(128)(2,1)} %param.16) | copy-start | bytes 36868
  54.4 246.3 %all-to-all-start.2 = ((bf16[32,192,1536]{2,1,0:T(8,128)(2,1)}), bf16[32,192,1536]{2,1,0:T(8,128)(2,1)}, u32[]{:S(2)}, u32[]{:S(2)}) async-start(bf16[32,192,1536]{2,1,0:T(8,128)(2,1)} %stack.2), calls=%async_computation.2 | async-start | bytes 37748736 | tf_op jit(solution)/shard_map/all_to_all | solution.py:96
  59.7 299.7 %all-reduce.2.cloned.1.call-start = ((), (), s32[]{:S(2)}) async-start(), calls=%async_computation.4 | async-start | bytes 327680 | tf_op jit(solution)/shard_map/psum | solution.py:103
  300.7 20.5 %copy-start.5 = (bf16[1536,128]{1,0:T(8,128)(2,1)S(1)}, bf16[1536,128]{1,0:T(8,128)(2,1)}, u32[]{:S(2)}) copy-start(bf16[1536,128]{1,0:T(8,128)(2,1)} %param.17) | copy-start | bytes 1179652
  319.3 1.9 copy-start.7
  321.3 39.1 %copy-start.6 = (bf16[640,128]{1,0:T(8,128)(2,1)S(1)}, bf16[640,128]{1,0:T(8,128)(2,1)}, u32[]{:S(2)}) copy-start(bf16[640,128]{1,0:T(8,128)(2,1)} %param.18) | copy-start | bytes 491524
  323.4 186.5 %reduce-scatter.2.cloned.1.call-start = ((), (), s32[]{:S(2)}) async-start(), calls=%async_computation.5 | async-start | bytes 19464192 | tf_op jit(solution)/shard_map/reduce_scatter | solution.py:112
  360.3 27.2 %copy-start.3 = (f32[640,128]{1,0:T(8,128)}, f32[640,128]{1,0:T(8,128)S(1)}, u32[]{:S(2)}) copy-start(f32[640,128]{1,0:T(8,128)S(1)} %convert_element_type.47) | copy-start | bytes 983044
  387.6 122.4 %copy-start.2 = (f32[192,1536]{1,0:T(8,128)S(1)}, f32[192,1536]{1,0:T(8,128)}, u32[]{:S(2)}) copy-start(f32[192,1536]{1,0:T(8,128)} %param.19) | copy-start | bytes 3538948
  387.6 126.8 %copy-start.1 = (bf16[128,6144]{1,0:T(8,128)(2,1)S(1)}, bf16[128,6144]{1,0:T(8,128)(2,1)}, u32[]{:S(2)}) copy-start(bf16[128,6144]{1,0:T(8,128)(2,1)} %param.15) | copy-start | bytes 4718596
Sparse Core Ops, SparseCore 0:
  323.6 35.7 all-reduce.1
  387.7 122.1 reduce-scatter.1
